TPU v7x, 128 devices: a whole 4x4x4 slice. The times are simulated.
128 devices in a mesh: occ: 4 (over y_hi, core), aux: 32 (over x, z, y_lo).
Axes of the slice: x: 4, y: 4 (y_hi: 2, y_lo: 2; y = y_hi * 2 + y_lo), z: 4, core: 2. Of those that a mesh axis runs over, the one named last changes fastest.
Arguments:
- three_index: bfloat16 [12000, 6, 1920], P('aux'), may hold values from -0.47851562 to 0.47851562
- occ_energy: float32 [6], replicated, may hold values from -1.5 to -0.3
- vir_energy: float32 [1920], replicated, may hold values from 0.25 to 2.95
- batch_table: int32 [6], replicated, may hold values from 0 to 5, each once
- orbital_order: int32 [6], replicated, may hold values from 0 to 5, each once
- occ_pair_int: bfloat16 [2, 2, 12000], P(None, None, 'aux'), may hold values from -0.03881836 to 0.03881836
- half_ao: bfloat16 [2, 12000, 4000], P(None, 'aux'), may hold values from -9.536743e-06 to 9.536743e-06
- vir_coeff: bfloat16 [4000, 1920], P('aux', 'occ'), may hold values from -0.09375 to 0.09375
Outputs:
- gamma: bfloat16 [12000, 2, 1920], P('aux', None, 'occ')
- orbital_gradient: float32 [2, 1920], P(None, ('occ', 'aux'))
Inputs may be any that keep to these rules, and one draw needn't show every extreme that they name: `batch_table`: a permutation of 0 to 5; its first 4 entries are the partner orbitals of the window. `orbital_order`: a permutation of 0 to 5; its first 2 entries are the orbitals whose amplitudes are formed.
All inputs are finite; a program needn't handle non-finite values.
Results may differ from a plain program's by a relative error of at most 0.019.
Values may be sent and summed in bfloat16 or wider, within the bound.
No kernel may reach another device: no remote copies, remote signals or barrier semaphores. Data moves between devices by JAX's collectives and lax.ppermute only.
A program may use at most 128 MiB of HBM per device.

v0:
```python
import jax
import jax.numpy as jnp
from jax import lax
from jax.sharding import Mesh
from jax.sharding import PartitionSpec as P

NI = 2
KH = 2
ROWS = 30
PAD = 32
AUX = ("x", "z", "yl")
OCC_AUX = ("yh", "core", "x", "z", "yl")
F32 = jnp.float32
BF16 = jnp.bfloat16


def ring(n, d):
    return [(i, (i + d) % n) for i in range(n)]


def up(v, axis):
    return lax.ppermute(v, axis, ring(4, 1))


def down(v, axis):
    return lax.ppermute(v, axis, ring(4, -1))


def dot(a, b, dims):
    return lax.dot_general(a, b, (dims, ((), ())), preferred_element_type=F32)


def ring_sum(v, axis):
    lo2, hi2 = v[2]
    got_up = up(lo2.astype(BF16), axis)
    got_down = down(hi2.astype(BF16), axis)
    one = jnp.concatenate([v[1][0] + got_up.astype(F32), v[1][1]]).astype(BF16)
    three = jnp.concatenate([v[3][0], v[3][1] + got_down.astype(F32)]).astype(BF16)
    from_below = up(one, axis)
    from_above = down(three, axis)
    own = jnp.concatenate([v[0][0], v[0][1]])
    return own + from_below.astype(F32) + from_above.astype(F32)


def ring_gather(v, axis):
    below = up(v, axis)
    above = down(v, axis)
    half = v.shape[0] // 2
    lo = up(below[:half], axis)
    hi = down(above[half:], axis)
    return [v, above, jnp.concatenate([lo, hi]), below]


def local(
    three_index,
    occ_energy,
    vir_energy,
    batch_table,
    orbital_order,
    occ_pair_int,
    half_ao,
    vir_coeff,
):
    nq, _, nvirt = three_index.shape
    yh, core, x, z, yl = (lax.axis_index(a) for a in OCC_AUX)
    own_a = (yh * 2 + core) * (nvirt // 4)
    by_orbital = jnp.transpose(three_index, (1, 0, 2))

    def orbital(i):
        return lax.dynamic_index_in_dim(by_orbital, i, 0, keepdims=False)

    def partner_orbital(half, k):
        return lax.dynamic_index_in_dim(batch_table, half * KH + k, 0, keepdims=False)

    pairs = []
    for h in range(2):
        for c in range(2):
            for t in range(2):
                src = h * 4 + c * 2 + t
                dst = (h if c == 0 else 1 - h) * 4 + c * 2 + (1 - t)
                pairs.append((src, dst))
    swap = lambda v: lax.ppermute(v, ("yh", "core", "yl"), pairs)
    right_sent = orbital(partner_orbital(1 - yl, core))
    right_first = swap(right_sent)
    right_second = lax.ppermute(right_first, "core", [(0, 1), (1, 0)])
    place = lax.broadcasted_iota(jnp.int32, (16 * PAD, 1), 0)
    dx, dz, r = (place // (4 * PAD), place // PAD % 4, place % PAD)
    chunk = (x + dx) % 4 * 4 + (z + dz) % 4
    virt = jnp.where(r < ROWS, chunk * ROWS + r, -nvirt)

    def left_rows(first):
        hot = (lax.broadcasted_iota(jnp.int32, (1, nvirt), 1) == virt + first).astype(BF16)
        both = [
            dot(hot, orbital(orbital_order[s]), ((1,), (1,))).astype(BF16).reshape(16, 1, PAD, nq)
            for s in range(NI)
        ]
        return jnp.concatenate(both, axis=1).reshape(16 * NI * PAD, nq)

    target_yh = jnp.where(core == 0, yh, 1 - yh)
    left_own = left_rows(own_a)
    left_sent = left_rows((target_yh * 2 + core) * (nvirt // 4))
    left_other = swap(left_sent)
    right_own = [orbital(partner_orbital(yl, k)) for k in range(KH)]
    right_other = [
        jnp.where(core == 0, right_first, right_second),
        jnp.where(core == 0, right_second, right_first),
    ]
    pair_flat = occ_pair_int.reshape(NI * NI, nq)
    g = [dot(pair_flat, half_ao[t], ((1,), (0,))) for t in range(NI)]
    cell = lambda u, v, t: g[t][u * NI + v]
    fock_terms = []
    for s in range(NI):
        fock_terms.append(2.0 * cell(0, 0, s) - cell(s, 0, 0))
        fock_terms.append(2.0 * (cell(0, 1, s) + cell(1, 0, s)) - cell(s, 1, 0) - cell(s, 0, 1))
        fock_terms.append(2.0 * cell(1, 1, s) - cell(s, 1, 1))
    fock_terms = jnp.stack(fock_terms)
    n_aux = lax.axis_size(AUX)
    tile = half_ao.shape[2] // n_aux
    fock_tile = lax.psum_scatter(
        fock_terms.reshape(6, n_aux, tile).transpose(1, 0, 2), AUX, scatter_dimension=0, tiled=False
    )
    vir_part = jnp.dot(fock_tile, vir_coeff.astype(F32), precision=lax.Precision.HIGHEST)
    share = vir_part.shape[1] // n_aux
    vir_own = lax.psum_scatter(
        vir_part.reshape(6, n_aux, share).transpose(1, 0, 2), AUX, scatter_dimension=0, tiled=False
    )
    pair_other = lax.ppermute(pair_flat, "yl", [(0, 1), (1, 0)])
    z_part = jnp.stack(
        [
            dot(pair_flat, right_own[k], ((1,), (0,)))
            + dot(pair_other, right_other[k], ((1,), (0,)))
            for k in range(KH)
        ]
    )
    z_sum = lax.psum(z_part, ("x", "z"))

    def by_block(left, swapped):
        blocks = left.reshape(4, 4, NI * PAD, nq)
        blocks = blocks.transpose(1, 0, 2, 3) if swapped else blocks
        return blocks.reshape(4, 2, 2 * NI * PAD, nq)

    summed = []
    for k, (first, second) in enumerate((("x", "z"), ("z", "x"))):
        lo_, oo_ = (by_block(left_own, k == 1), by_block(left_other, k == 1))
        v = {}
        for d in (2, 1, 3, 0):
            v[d] = [
                dot(lo_[d, h], right_own[k], ((1,), (0,)))
                + dot(oo_[d, h], right_other[k], ((1,), (0,)))
                for h in range(2)
            ]
        u = ring_sum(v, first).reshape(4, 2, PAD, nvirt)
        w = ring_sum([[u[d, 0], u[d, 1]] for d in range(4)], second)
        summed.append(w.reshape(NI, PAD, nvirt))
    own_chunk = x * 4 + z
    padded = jnp.concatenate([vir_energy, vir_energy[:2]])
    row_energy = lax.dynamic_slice_in_dim(padded, own_a + own_chunk * ROWS, PAD)
    left_energy = jnp.stack([occ_energy[orbital_order[s]] for s in range(NI)])
    amps = []
    for k in range(KH):
        e_k = lax.dynamic_index_in_dim(occ_energy, partner_orbital(yl, k), 0, keepdims=False)
        denominator = (
            row_energy[None, :, None] + vir_energy[None, None, :] - left_energy[:, None, None] - e_k
        )
        amps.append((-summed[k] / denominator).astype(BF16))
    wide = [a.astype(F32) for a in amps]
    entries = [-sum((jnp.sum(w[s] * w[t]) for w in wide)) for s, t in ((0, 0), (0, 1), (1, 1))]
    density = lax.psum(jnp.stack(entries), OCC_AUX)
    occ_rows = []
    for s in range(NI):
        row = jnp.zeros((PAD,), F32)
        for k in range(KH):
            for u in range(NI):
                row = row - jnp.sum(wide[k][u] * z_sum[k, u * NI + s][None, :], axis=1)
        occ_rows.append(row)
    occ_rows = jnp.stack(occ_rows)
    mine = lax.dynamic_slice_in_dim(occ_rows, yl * share, share, axis=1)
    theirs = lax.dynamic_slice_in_dim(occ_rows, (1 - yl) * share, share, axis=1)
    occ_side = mine + lax.ppermute(theirs, "yl", [(0, 1), (1, 0)])
    gammas = []
    for k, (first, second) in enumerate((("z", "x"), ("x", "z"))):
        own = jnp.concatenate(ring_gather(amps[k].reshape(NI * PAD, nvirt), first))
        blocks = ring_gather(own, second)
        parts = [
            [dot(b, right[k], ((1,), (1,))) for b in blocks] for right in (right_other, right_own)
        ]
        both = [jnp.concatenate(p).reshape(4, 4, NI * PAD, nq) for p in parts]
        if k == 1:
            both = [b.transpose(1, 0, 2, 3) for b in both]
        gammas.append(both)
    gamma_sent = (gammas[0][0] + gammas[1][0]).astype(BF16)
    gamma_got = lax.ppermute(gamma_sent, "yl", [(0, 1), (1, 0)])
    gamma_rows = (gammas[0][1] + gammas[1][1] + gamma_got.astype(F32)).astype(BF16)
    gamma_rows = gamma_rows.reshape(16, NI, PAD, nq)
    target = lax.broadcasted_iota(jnp.int32, (nvirt // 4, 1), 0)
    back = (target == virt.reshape(1, 16 * PAD)).astype(BF16)
    gamma_out = jnp.stack(
        [
            dot(back, gamma_rows[:, s].reshape(16 * PAD, nq), ((1,), (0,))).astype(BF16)
            for s in range(NI)
        ]
    )
    gamma_out = jnp.transpose(gamma_out, (2, 0, 1))
    weights = vir_own.reshape(NI, 3, share)
    gradient = occ_side + jnp.sum(weights * density[None, :, None], axis=1)
    return (gamma_out, gradient)


def solution(mesh):
    torus = Mesh(mesh.devices.reshape(2, 2, 4, 4, 2), OCC_AUX)
    occ = ("yh", "core")
    return jax.shard_map(
        local,
        mesh=torus,
        in_specs=(
            P(AUX, None, None),
            P(),
            P(),
            P(),
            P(),
            P(None, None, AUX),
            P(None, AUX, None),
            P(AUX, occ),
        ),
        out_specs=(P(AUX, None, occ), P(None, OCC_AUX)),
        check_vma=False,
    )
```

profile of v0, /device:TPU:0, one launch (start us, length us, event | category | flops | bytes accessed | tf_op | source)
XLA Modules:
  0.0 838.8 jit_solution(4391718574668692102)
XLA Ops:
  10.5 2.6 dynamic-slice_bitcast_fusion
  18.5 2.5 fusion.101
  21.8 2.5 fusion.104
  28.3 13.4 %fusion.165 = (bf16[1,375,4000]{2,0,1:T(2,128)(2,1)}, bf16[1,375,4000]{2,0,1:T(2,128)(2,1)}) fusion(bf16[2,375,4000]{2,0,1:T(2,128)(2,1)} %param.14), kind=kLoop, calls=%fused_computation.334 | loop fusion | bytes 12000000 | tf_op jit(solution)/shard_map/slice | solution.py:109
  41.7 13.8 %copy.135 = bf16[1,375,4000]{1,2,0:T(8,128)(2,1)S(1)} copy(bf16[1,375,4000]{2,0,1:T(2,128)(2,1)} %get-tuple-element.35) | data formatting | bytes 6000000
  56.4 13.9 %copy.134 = bf16[1,375,4000]{1,2,0:T(8,128)(2,1)S(1)} copy(bf16[1,375,4000]{2,0,1:T(2,128)(2,1)} %get-tuple-element.34) | data formatting | bytes 6000000
  74.2 2.5 fusion.95
  80.5 2.8 fusion.79
  83.3 2.8 fusion.81
  86.0 2.7 fusion.77
  88.8 2.7 fusion.71
  91.5 2.7 fusion.73
  94.2 2.7 fusion.75
  97.0 2.8 fusion.83
  99.7 2.7 fusion.85
  104.5 2.7 fusion.53
  107.2 2.8 fusion.55
  111.6 2.8 fusion.51
  114.5 2.8 fusion.45
  117.3 2.7 fusion.47
  120.0 2.8 fusion.49
  122.8 2.8 fusion.59
  128.4 2.8 fusion.57
  133.1 221.0 %all-reduce.4.cloned.1.call-done = f32[32,6,125]{2,1,0:T(8,128)} async-done(((f32[32,6,125]{2,1,0:T(8,128)}), f32[32,6,125]{2,1,0:T(8,128)}) %all-reduce.4.cloned.1.call-update) | async-done | bytes 96016
  356.1 154.6 %all-reduce.1 = f32[32,6,15]{2,1,0:T(8,128)S(1)} all-reduce(f32[32,6,15]{2,1,0:T(8,128)S(1)} %copy.133), channel_id=3, replica_groups=mesh['yh'=2,'core'=2,'x'=4,'z'=4,'yl'=2] {'x','z','yl'}, use_global_device_ids=true, to_apply=%region_10.11.clone | all-reduce | flops 2880 | bytes 23040
  519.9 3.2 collective-permute-start.5
  530.9 3.2 collective-permute-start.21
  537.5 70.3 %psum.14 = f32[2,4,1920]{2,1,0:T(4,128)S(1)} all-reduce(f32[2,4,1920]{2,1,0:T(4,128)S(1)} %pad_maximum_fusion.14), channel_id=1, replica_groups=mesh['yh'=2,'core'=2,'x'=4,'z'=4,'yl'=2] {'x','z'}, use_global_device_ids=true, to_apply=%region_0.1 | all-reduce | flops 15360 | bytes 122880 | tf_op jit(solution)/shard_map/psum | solution.py:135
  620.9 2.7 collective-permute-start.22
  623.5 3.2 collective-permute-done.4
  628.8 3.2 collective-permute-start.9
  635.7 3.2 collective-permute-start.25
  639.1 3.8 collective-permute-start.10
  643.1 3.3 collective-permute-start.26
  646.9 3.5 collective-permute-done.24
  654.3 3.3 collective-permute-start.27
  658.4 2.6 collective-permute-start.11
  668.1 65.9 %psum.15 = f32[3]{0:T(128)S(1)} all-reduce(f32[3]{0:T(128)S(1)} %pad_maximum_fusion.17), channel_id=1, replica_groups=mesh['yh'=2,'core'=2,'x'=4,'z'=4,'yl'=2] {'yh','core','x','z','yl'}, use_global_device_ids=true, to_apply=%region_17.18 | all-reduce | flops 3 | bytes 24 | tf_op jit(solution)/shard_map/psum | solution.py:168
  752.1 2.6 collective-permute-start.31
  758.3 2.7 collective-permute-start.15
  761.0 3.1 fusion.43
  764.1 2.9 fusion.69
  768.2 7.1 collective-permute-done.32
  775.6 3.3 collective-permute-start.34
  782.7 3.2 collective-permute-start.18
  805.9 3.0 copy.121
  808.9 2.6 fusion.32
  821.3 6.9 collective-permute-done.35
  (298 shorter events, 130.5 us)
Async XLA Ops:
  7.2 7.6 copy-start.42
  7.2 347.0 %all-reduce.4.cloned.1.call-start = ((), (), s32[]{:S(2)}) async-start(), calls=%async_computation | async-start | bytes 262144
  13.1 112.5 %collective-permute-start.1 = (bf16[375,1920]{1,0:T(8,128)(2,1)}, bf16[375,1920]{1,0:T(8,128)(2,1)}, u32[]{:S(2)}, u32[]{:S(2)}) collective-permute-start(bf16[375,1920]{1,0:T(8,128)(2,1)} %dynamic-slice_bitcast_fusion), channel_id=1, source_target_pairs={{0,1},{1,0},{32,97},{33,96},{64,65},{65,64},{96,33},{97,32},{2,3},... | collective-permute-start | bytes 4320008 | tf_op jit(solution)/shard_map/ppermute | solution.py:82
  26.0 485.3 %collective-permute-start = (bf16[1024,375]{0,1:T(8,128)(2,1)}, bf16[1024,375]{0,1:T(8,128)(2,1)}, u32[]{:S(2)}, u32[]{:S(2)}) collective-permute-start(bf16[1024,375]{0,1:T(8,128)(2,1)} %copy.104), channel_id=1, source_target_pairs={{0,1},{1,0},{32,97},{33,96},{64,65},{65,64},{96,33},{97,32},{2,3},... | collective-permute-start | bytes 2304008 | tf_op jit(solution)/shard_map/ppermute | solution.py:82
  26.4 510.5 %collective-permute-start.36 = (bf16[4,375]{1,0:T(4,128)(2,1)S(1)}, bf16[4,375]{1,0:T(4,128)(2,1)S(1)}, u32[]{:S(2)}, u32[]{:S(2)}) collective-permute-start(bf16[4,375]{1,0:T(4,128)(2,1)S(1)} %reshape.436), channel_id=1, source_target_pairs={{0,1},{1,0},{2,3},{3,2},{4,5},{5,4},{6,7},{7,6},{8,9},{9,8},{10,11... | collective-permute-start | bytes 9008 | tf_op jit(solution)/shard_map/ppermute | solution.py:127
  125.6 388.0 %collective-permute-start.2 = (bf16[375,1920]{1,0:T(8,128)(2,1)}, bf16[375,1920]{1,0:T(8,128)(2,1)}, u32[]{:S(2)}, u32[]{:S(2)}) collective-permute-start(bf16[375,1920]{1,0:T(8,128)(2,1)} %collective-permute-done.1), channel_id=1, source_target_pairs={{0,32},{32,0},{1,33},{33,1},{2,34},{34,2},{3,35},{35,3},{4,36},{36... | collective-permute-start | bytes 4320008 | tf_op jit(solution)/shard_map/ppermute | solution.py:85
  513.6 21.9 %copy-start.25 = (bf16[4,4,64,375]{3,2,1,0:T(8,128)(2,1)}, bf16[4,4,64,375]{3,2,1,0:T(8,128)(2,1)S(1)}, u32[]{:S(2)}) copy-start(bf16[4,4,64,375]{3,2,1,0:T(8,128)(2,1)S(1)} %copy.118) | copy-start | bytes 2304004
  517.5 92.3 %collective-permute-start.3 = (bf16[128,1920]{1,0:T(8,128)(2,1)}, bf16[128,1920]{1,0:T(8,128)(2,1)}, u32[]{:S(2)}, u32[]{:S(2)}) collective-permute-start(bf16[128,1920]{1,0:T(8,128)(2,1)} %fusion.13), channel_id=1, source_target_pairs={{0,8},{8,16},{16,24},{24,0},{1,9},{9,17},{17,25},{25,1},{2,10},{10... | collective-permute-start | bytes 1474568 | tf_op jit(solution)/shard_map/ppermute | solution.py:22
  519.9 91.6 %collective-permute-start.5 = (bf16[128,1920]{1,0:T(8,128)(2,1)}, bf16[128,1920]{1,0:T(8,128)(2,1)}, u32[]{:S(2)}, u32[]{:S(2)}) collective-permute-start(bf16[128,1920]{1,0:T(8,128)(2,1)} %fusion.17), channel_id=1, source_target_pairs={{0,24},{8,0},{16,8},{24,16},{1,25},{9,1},{17,9},{25,17},{2,26},{10... | collective-permute-start | bytes 1474568 | tf_op jit(solution)/shard_map/ppermute | solution.py:26
  528.4 88.1 %collective-permute-start.19 = (bf16[128,1920]{1,0:T(8,128)(2,1)}, bf16[128,1920]{1,0:T(8,128)(2,1)}, u32[]{:S(2)}, u32[]{:S(2)}) collective-permute-start(bf16[128,1920]{1,0:T(8,128)(2,1)} %fusion.19), channel_id=1, source_target_pairs={{0,2},{2,4},{4,6},{6,0},{1,3},{3,5},{5,7},{7,1},{8,10},{10,12},{12... | collective-permute-start | bytes 1474568 | tf_op jit(solution)/shard_map/ppermute | solution.py:22
  530.9 87.7 %collective-permute-start.21 = (bf16[128,1920]{1,0:T(8,128)(2,1)}, bf16[128,1920]{1,0:T(8,128)(2,1)}, u32[]{:S(2)}, u32[]{:S(2)}) collective-permute-start(bf16[128,1920]{1,0:T(8,128)(2,1)} %fusion.23), channel_id=1, source_target_pairs={{0,6},{2,0},{4,2},{6,4},{1,7},{3,1},{5,3},{7,5},{8,14},{10,8},{12,... | collective-permute-start | bytes 1474568 | tf_op jit(solution)/shard_map/ppermute | solution.py:26
  611.4 15.4 %collective-permute-start.4 = (bf16[256,1920]{1,0:T(8,128)(2,1)S(1)}, bf16[256,1920]{1,0:T(8,128)(2,1)S(1)}, u32[]{:S(2)}, u32[]{:S(2)}) collective-permute-start(bf16[256,1920]{1,0:T(8,128)(2,1)S(1)} %pad_maximum_fusion.4), channel_id=1, source_target_pairs={{0,8},{8,16},{16,24},{24,0},{1,9},{9,17},{17,25},{25,1},{2,10},{10... | collective-permute-start | bytes 2949128 | tf_op jit(solution)/shard_map/ppermute | solution.py:22
  614.1 14.2 %collective-permute-start.6 = (bf16[256,1920]{1,0:T(8,128)(2,1)S(1)}, bf16[256,1920]{1,0:T(8,128)(2,1)S(1)}, u32[]{:S(2)}, u32[]{:S(2)}) collective-permute-start(bf16[256,1920]{1,0:T(8,128)(2,1)S(1)} %pad_maximum_fusion.5), channel_id=1, source_target_pairs={{0,24},{8,0},{16,8},{24,16},{1,25},{9,1},{17,9},{25,17},{2,26},{10... | collective-permute-start | bytes 2949128 | tf_op jit(solution)/shard_map/ppermute | solution.py:26
  618.1 15.8 %collective-permute-start.20 = (bf16[256,1920]{1,0:T(8,128)(2,1)S(1)}, bf16[256,1920]{1,0:T(8,128)(2,1)S(1)}, u32[]{:S(2)}, u32[]{:S(2)}) collective-permute-start(bf16[256,1920]{1,0:T(8,128)(2,1)S(1)} %pad_maximum_fusion.6), channel_id=1, source_target_pairs={{0,2},{2,4},{4,6},{6,0},{1,3},{3,5},{5,7},{7,1},{8,10},{10,12},{12... | collective-permute-start | bytes 2949128 | tf_op jit(solution)/shard_map/ppermute | solution.py:22
  620.8 7.6 copy-start.23
  620.8 7.5 copy-start.24
  620.9 14.3 %collective-permute-start.22 = (bf16[256,1920]{1,0:T(8,128)(2,1)S(1)}, bf16[256,1920]{1,0:T(8,128)(2,1)S(1)}, u32[]{:S(2)}, u32[]{:S(2)}) collective-permute-start(bf16[256,1920]{1,0:T(8,128)(2,1)S(1)} %pad_maximum_fusion.7), channel_id=1, source_target_pairs={{0,6},{2,0},{4,2},{6,4},{1,7},{3,1},{5,3},{7,5},{8,14},{10,8},{12,... | collective-permute-start | bytes 2949128 | tf_op jit(solution)/shard_map/ppermute | solution.py:26
  628.7 6.5 copy-start.20
  628.8 10.1 %collective-permute-start.7 = (bf16[32,1920]{1,0:T(8,128)(2,1)S(1)}, bf16[32,1920]{1,0:T(8,128)(2,1)S(1)}, u32[]{:S(2)}, u32[]{:S(2)}) collective-permute-start(bf16[32,1920]{1,0:T(8,128)(2,1)S(1)} %get-tuple-element.50), channel_id=1, source_target_pairs={{0,2},{2,4},{4,6},{6,0},{1,3},{3,5},{5,7},{7,1},{8,10},{10,12},{12... | collective-permute-start | bytes 368648 | tf_op jit(solution)/shard_map/ppermute | solution.py:22
  628.8 10.1 %collective-permute-start.9 = (bf16[32,1920]{1,0:T(8,128)(2,1)S(1)}, bf16[32,1920]{1,0:T(8,128)(2,1)S(1)}, u32[]{:S(2)}, u32[]{:S(2)}) collective-permute-start(bf16[32,1920]{1,0:T(8,128)(2,1)S(1)} %get-tuple-element.51), channel_id=1, source_target_pairs={{0,6},{2,0},{4,2},{6,4},{1,7},{3,1},{5,3},{7,5},{8,14},{10,8},{12,... | collective-permute-start | bytes 368648 | tf_op jit(solution)/shard_map/ppermute | solution.py:26
  635.6 7.3 collective-permute-start.23
  635.7 7.2 collective-permute-start.25
  639.0 7.9 collective-permute-start.8
  639.1 7.8 collective-permute-start.10
  643.0 7.5 collective-permute-start.24
  643.1 7.4 collective-permute-start.26
  654.3 83.3 %collective-permute-start.27 = (bf16[64,1920]{1,0:T(8,128)(2,1)}, bf16[64,1920]{1,0:T(8,128)(2,1)}, u32[]{:S(2)}, u32[]{:S(2)}) collective-permute-start(bf16[64,1920]{1,0:T(8,128)(2,1)} %get-tuple-element.30), channel_id=1, source_target_pairs={{0,24},{8,0},{16,8},{24,16},{1,25},{9,1},{17,9},{25,17},{2,26},{10... | collective-permute-start | bytes 737288 | tf_op jit(solution)/shard_map/ppermute | solution.py:26
  657.7 77.1 %collective-permute-start.28 = (bf16[64,1920]{1,0:T(8,128)(2,1)}, bf16[64,1920]{1,0:T(8,128)(2,1)}, u32[]{:S(2)}, u32[]{:S(2)}) collective-permute-start(bf16[64,1920]{1,0:T(8,128)(2,1)} %get-tuple-element.30), channel_id=1, source_target_pairs={{0,8},{8,16},{16,24},{24,0},{1,9},{9,17},{17,25},{25,1},{2,10},{10... | collective-permute-start | bytes 737288 | tf_op jit(solution)/shard_map/ppermute | solution.py:22
  658.4 84.4 %collective-permute-start.11 = (bf16[64,1920]{1,0:T(8,128)(2,1)S(1)}, bf16[64,1920]{1,0:T(8,128)(2,1)}, u32[]{:S(2)}, u32[]{:S(2)}) collective-permute-start(bf16[64,1920]{1,0:T(8,128)(2,1)S(1)} %get-tuple-element.58), channel_id=1, source_target_pairs={{0,6},{2,0},{4,2},{6,4},{1,7},{3,1},{5,3},{7,5},{8,14},{10,8},{12,... | collective-permute-start | bytes 737288 | tf_op jit(solution)/shard_map/ppermute | solution.py:26
  661.0 79.0 %collective-permute-start.12 = (bf16[64,1920]{1,0:T(8,128)(2,1)S(1)}, bf16[64,1920]{1,0:T(8,128)(2,1)}, u32[]{:S(2)}, u32[]{:S(2)}) collective-permute-start(bf16[64,1920]{1,0:T(8,128)(2,1)S(1)} %get-tuple-element.58), channel_id=1, source_target_pairs={{0,2},{2,4},{4,6},{6,0},{1,3},{3,5},{5,7},{7,1},{8,10},{10,12},{12... | collective-permute-start | bytes 737288 | tf_op jit(solution)/shard_map/ppermute | solution.py:22
  668.1 66.0 %collective-permute-start.37 = (f32[2,15]{1,0:T(2,128)S(1)}, f32[2,15]{1,0:T(2,128)S(1)}, u32[]{:S(2)}, u32[]{:S(2)}) collective-permute-start(f32[2,15]{1,0:T(2,128)S(1)} %constant_dynamic-slice_fusion), channel_id=1, source_target_pairs={{0,1},{1,0},{2,3},{3,2},{4,5},{5,4},{6,7},{7,6},{8,9},{9,8},{10,11... | collective-permute-start | bytes 368 | tf_op jit(solution)/shard_map/ppermute | solution.py:179
  735.7 12.8 %collective-permute-start.29 = (bf16[32,1920]{1,0:T(8,128)(2,1)S(1)}, bf16[32,1920]{1,0:T(8,128)(2,1)S(1)}, u32[]{:S(2)}, u32[]{:S(2)}) collective-permute-start(bf16[32,1920]{1,0:T(8,128)(2,1)S(1)} %slice.420), channel_id=1, source_target_pairs={{0,8},{8,16},{16,24},{24,0},{1,9},{9,17},{17,25},{25,1},{2,10},{10... | collective-permute-start | bytes 368648 | tf_op jit(solution)/shard_map/ppermute | solution.py:22
  738.5 10.6 %collective-permute-start.30 = (bf16[32,1920]{1,0:T(8,128)(2,1)S(1)}, bf16[32,1920]{1,0:T(8,128)(2,1)S(1)}, u32[]{:S(2)}, u32[]{:S(2)}) collective-permute-start(bf16[32,1920]{1,0:T(8,128)(2,1)S(1)} %slice.421), channel_id=1, source_target_pairs={{0,24},{8,0},{16,8},{24,16},{1,25},{9,1},{17,9},{25,17},{2,26},{10... | collective-permute-start | bytes 368648 | tf_op jit(solution)/shard_map/ppermute | solution.py:26
  740.9 13.8 %collective-permute-start.13 = (bf16[32,1920]{1,0:T(8,128)(2,1)S(1)}, bf16[32,1920]{1,0:T(8,128)(2,1)S(1)}, u32[]{:S(2)}, u32[]{:S(2)}) collective-permute-start(bf16[32,1920]{1,0:T(8,128)(2,1)S(1)} %slice.392), channel_id=1, source_target_pairs={{0,2},{2,4},{4,6},{6,0},{1,3},{3,5},{5,7},{7,1},{8,10},{10,12},{12... | collective-permute-start | bytes 368648 | tf_op jit(solution)/shard_map/ppermute | solution.py:22
  743.7 11.6 %collective-permute-start.14 = (bf16[32,1920]{1,0:T(8,128)(2,1)S(1)}, bf16[32,1920]{1,0:T(8,128)(2,1)S(1)}, u32[]{:S(2)}, u32[]{:S(2)}) collective-permute-start(bf16[32,1920]{1,0:T(8,128)(2,1)S(1)} %slice.393), channel_id=1, source_target_pairs={{0,6},{2,0},{4,2},{6,4},{1,7},{3,1},{5,3},{7,5},{8,14},{10,8},{12,... | collective-permute-start | bytes 368648 | tf_op jit(solution)/shard_map/ppermute | solution.py:26
  751.4 23.9 %collective-permute-start.32 = (bf16[256,1920]{1,0:T(8,128)(2,1)}, bf16[256,1920]{1,0:T(8,128)(2,1)S(1)}, u32[]{:S(2)}, u32[]{:S(2)}) collective-permute-start(bf16[256,1920]{1,0:T(8,128)(2,1)} %constant_dynamic-update-slice_fusion.7), channel_id=1, source_target_pairs={{0,2},{2,4},{4,6},{6,0},{1,3},{3,5},{5,7},{7,1},{8,10},{10,12},{12... | collective-permute-start | bytes 2949128 | tf_op jit(solution)/shard_map/ppermute | solution.py:22
  752.1 23.4 %collective-permute-start.31 = (bf16[256,1920]{1,0:T(8,128)(2,1)}, bf16[256,1920]{1,0:T(8,128)(2,1)S(1)}, u32[]{:S(2)}, u32[]{:S(2)}) collective-permute-start(bf16[256,1920]{1,0:T(8,128)(2,1)} %constant_dynamic-update-slice_fusion.7), channel_id=1, source_target_pairs={{0,6},{2,0},{4,2},{6,4},{1,7},{3,1},{5,3},{7,5},{8,14},{10,8},{12,... | collective-permute-start | bytes 2949128 | tf_op jit(solution)/shard_map/ppermute | solution.py:26
  757.6 6.5 copy-start.6
  757.6 23.4 %collective-permute-start.16 = (bf16[256,1920]{1,0:T(8,128)(2,1)}, bf16[256,1920]{1,0:T(8,128)(2,1)S(1)}, u32[]{:S(2)}, u32[]{:S(2)}) collective-permute-start(bf16[256,1920]{1,0:T(8,128)(2,1)} %constant_dynamic-update-slice_fusion), channel_id=1, source_target_pairs={{0,8},{8,16},{16,24},{24,0},{1,9},{9,17},{17,25},{25,1},{2,10},{10... | collective-permute-start | bytes 2949128 | tf_op jit(solution)/shard_map/ppermute | solution.py:22
  758.3 23.5 %collective-permute-start.15 = (bf16[256,1920]{1,0:T(8,128)(2,1)}, bf16[256,1920]{1,0:T(8,128)(2,1)S(1)}, u32[]{:S(2)}, u32[]{:S(2)}) collective-permute-start(bf16[256,1920]{1,0:T(8,128)(2,1)} %constant_dynamic-update-slice_fusion), channel_id=1, source_target_pairs={{0,24},{8,0},{16,8},{24,16},{1,25},{9,1},{17,9},{25,17},{2,26},{10... | collective-permute-start | bytes 2949128 | tf_op jit(solution)/shard_map/ppermute | solution.py:26
  761.0 6.0 copy-start.5
  764.1 25.7 %slice-start = ((s8[8663040]{0:T(1024)(128)(4,1)}), s8[4194304]{0:T(1024)(128)(4,1)S(1)}, s32[]{:S(2)}) async-start(s8[8663040]{0:T(1024)(128)(4,1)} %bitcast.415), calls=%async_computation.1 | async-start | bytes 8388608
  767.6 22.3 %slice-start.1 = ((s8[8663040]{0:T(1024)(128)(4,1)}), s8[4194304]{0:T(1024)(128)(4,1)S(1)}, s32[]{:S(2)}) async-start(s8[8663040]{0:T(1024)(128)(4,1)} %bitcast.415), calls=%async_computation.2 | async-start | bytes 8388608
  775.4 20.0 %collective-permute-start.33 = (bf16[128,1920]{1,0:T(8,128)(2,1)S(1)}, bf16[128,1920]{1,0:T(8,128)(2,1)S(1)}, u32[]{:S(2)}, u32[]{:S(2)}) collective-permute-start(bf16[128,1920]{1,0:T(8,128)(2,1)S(1)} %slice.422), channel_id=1, source_target_pairs={{0,2},{2,4},{4,6},{6,0},{1,3},{3,5},{5,7},{7,1},{8,10},{10,12},{12... | collective-permute-start | bytes 1474568 | tf_op jit(solution)/shard_map/ppermute | solution.py:22
  775.6 19.9 %collective-permute-start.34 = (bf16[128,1920]{1,0:T(8,128)(2,1)S(1)}, bf16[128,1920]{1,0:T(8,128)(2,1)S(1)}, u32[]{:S(2)}, u32[]{:S(2)}) collective-permute-start(bf16[128,1920]{1,0:T(8,128)(2,1)S(1)} %slice.423), channel_id=1, source_target_pairs={{0,6},{2,0},{4,2},{6,4},{1,7},{3,1},{5,3},{7,5},{8,14},{10,8},{12,... | collective-permute-start | bytes 1474568 | tf_op jit(solution)/shard_map/ppermute | solution.py:26
  781.8 18.4 %collective-permute-start.17 = (bf16[128,1920]{1,0:T(8,128)(2,1)}, bf16[128,1920]{1,0:T(8,128)(2,1)}, u32[]{:S(2)}, u32[]{:S(2)}) collective-permute-start(bf16[128,1920]{1,0:T(8,128)(2,1)} %slice.394), channel_id=1, source_target_pairs={{0,8},{8,16},{16,24},{24,0},{1,9},{9,17},{17,25},{25,1},{2,10},{10... | collective-permute-start | bytes 1474568 | tf_op jit(solution)/shard_map/ppermute | solution.py:22
  782.7 18.7 %collective-permute-start.18 = (bf16[128,1920]{1,0:T(8,128)(2,1)}, bf16[128,1920]{1,0:T(8,128)(2,1)}, u32[]{:S(2)}, u32[]{:S(2)}) collective-permute-start(bf16[128,1920]{1,0:T(8,128)(2,1)} %slice.395), channel_id=1, source_target_pairs={{0,24},{8,0},{16,8},{24,16},{1,25},{9,1},{17,9},{25,17},{2,26},{10... | collective-permute-start | bytes 1474568 | tf_op jit(solution)/shard_map/ppermute | solution.py:26
  811.5 16.8 %collective-permute-start.35 = (bf16[4,4,64,375]{3,2,1,0:T(8,128)(2,1)}, bf16[4,4,64,375]{3,2,1,0:T(8,128)(2,1)}, u32[]{:S(2)}, u32[]{:S(2)}) collective-permute-start(bf16[4,4,64,375]{3,2,1,0:T(8,128)(2,1)} %fusion.32), channel_id=1, source_target_pairs={{0,1},{1,0},{2,3},{3,2},{4,5},{5,4},{6,7},{7,6},{8,9},{9,8},{10,11... | collective-permute-start | bytes 2304008 | tf_op jit(solution)/shard_map/ppermute | solution.py:192
  (39 other events, 100.8 us)
Sparse Core Ops, SparseCore 0:
  73.1 280.9 all-reduce.3
where the time goes:
time: 845 us; the launch traced here: 839 us
  blocking collectives  291 us (34%)
  waiting for transfers between devices  249 us (29%)
  matrix products  107 us (13%)
  local copies, waits for them, and re-layouts  85.2 us (10%)
  starting transfers between devices  57.4 us (7%)
  between operations  28.5 us (3%)
  other arithmetic  21.1 us (2%)
    unnamed x2, waiting for transfers between devices  221 us
    unnamed x1, blocking collectives  155 us
    dot_general x60, matrix products, dot(): return lax.dot_general(a, b, (dims, ((), ())), preferred_element_type=F32)  105 us
    psum x1, blocking collectives, local(): z_sum = lax.psum(z_part, ('x', 'z'))  70.3 us
    psum x1, blocking collectives, local(): density = lax.psum(jnp.stack(entries), OCC_AUX)  65.9 us
    ppermute x16, starting transfers between devices, down(): return lax.ppermute(v, axis, ring(4, -1))  45.5 us
    unnamed x108, local copies, waits for them, and re-layouts  43.4 us
    ppermute x16, waiting for transfers between devices, up(): return lax.ppermute(v, axis, ring(4, 1))  18.4 us
  transfers between devices with their start and end apart: 39, of which 10 were waited for; matrix products, arithmetic and copies ran while one was open for 22% of the time, Pallas kernels for 0%

commit v1 on v0

--- a/solution.py
+++ b/solution.py
@@ -132,7 +132,8 @@
             for k in range(KH)
         ]
     )
-    z_sum = lax.psum(z_part, ("x", "z"))
+    remake_sites = lambda sample: lax.psum(lax.psum(sample, axis_name="x"), axis_name="z")
+    z_sum = remake_sites(z_part)
 
     def by_block(left, swapped):
         blocks = left.reshape(4, 4, NI * PAD, nq)

time: 845 us -> 805 us (0.953)
  blocking collectives: 291 us -> 250 us
    psum x1 -> x2, blocking collectives: 70.3 us -> 30.1 us  [the longest x1 15.1 us: local(): lax.psum(lax.psum(sample, axis_name='x'), axis_name='z')]
  transfers between devices with their start and end apart: 39 -> 39, of which waited for: 10 -> 10; matrix products, arithmetic and copies ran while one was open for 22% -> 24% of each run, Pallas kernels for 0% -> 0%
where the time goes in v1:
time: 805 us; the launch traced here: 799 us
  blocking collectives  250 us (31%)
  waiting for transfers between devices  249 us (31%)
  matrix products  107 us (13%)
  local copies, waits for them, and re-layouts  84.5 us (10%)
  starting transfers between devices  58.3 us (7%)
  between operations  29 us (4%)
  other arithmetic  21.3 us (3%)
    unnamed x2, waiting for transfers between devices  221 us
    unnamed x1, blocking collectives  155 us
    dot_general x60, matrix products, dot(): return lax.dot_general(a, b, (dims, ((), ())), preferred_element_type=F32)  105 us
    psum x1, blocking collectives, local(): density = lax.psum(jnp.stack(entries), OCC_AUX)  65.5 us
    ppermute x16, starting transfers between devices, down(): return lax.ppermute(v, axis, ring(4, -1))  44.7 us
    unnamed x108, local copies, waits for them, and re-layouts  42.7 us
    ppermute x16, waiting for transfers between devices, up(): return lax.ppermute(v, axis, ring(4, 1))  19.2 us
  transfers between devices with their start and end apart: 39, of which 10 were waited for; matrix products, arithmetic and copies ran while one was open for 24% of the time, Pallas kernels for 0%

profile of v1, /device:TPU:0, one launch (start us, length us, event | category | flops | bytes accessed | tf_op | source)
XLA Modules:
  0.0 798.9 jit_solution(13886760663906269118)
XLA Ops:
  10.6 2.6 dynamic-slice_bitcast_fusion
  18.7 2.5 fusion.101
  28.6 13.4 %fusion.165 = (bf16[1,375,4000]{2,0,1:T(2,128)(2,1)}, bf16[1,375,4000]{2,0,1:T(2,128)(2,1)}) fusion(bf16[2,375,4000]{2,0,1:T(2,128)(2,1)} %param.14), kind=kLoop, calls=%fused_computation.334 | loop fusion | bytes 12000000 | tf_op jit(solution)/shard_map/slice | solution.py:109
  42.0 13.8 %copy.135 = bf16[1,375,4000]{1,2,0:T(8,128)(2,1)S(1)} copy(bf16[1,375,4000]{2,0,1:T(2,128)(2,1)} %get-tuple-element.35) | data formatting | bytes 6000000
  56.8 13.9 %copy.134 = bf16[1,375,4000]{1,2,0:T(8,128)(2,1)S(1)} copy(bf16[1,375,4000]{2,0,1:T(2,128)(2,1)} %get-tuple-element.34) | data formatting | bytes 6000000
  77.3 2.5 fusion.98
  81.2 2.8 fusion.79
  84.0 2.7 fusion.81
  86.7 2.7 fusion.77
  89.5 2.7 fusion.71
  92.2 2.7 fusion.73
  94.9 2.7 fusion.75
  97.7 2.7 fusion.83
  100.4 2.7 fusion.85
  105.2 2.8 fusion.53
  107.9 2.8 fusion.55
  112.4 2.8 fusion.51
  115.2 2.8 fusion.45
  118.0 2.7 fusion.47
  120.7 2.8 fusion.49
  123.5 2.8 fusion.59
  129.1 2.7 fusion.57
  134.0 220.5 %all-reduce.4.cloned.1.call-done = f32[32,6,125]{2,1,0:T(8,128)} async-done(((f32[32,6,125]{2,1,0:T(8,128)}), f32[32,6,125]{2,1,0:T(8,128)}) %all-reduce.4.cloned.1.call-update) | async-done | bytes 96016
  356.5 154.6 %all-reduce.1 = f32[32,6,15]{2,1,0:T(8,128)S(1)} all-reduce(f32[32,6,15]{2,1,0:T(8,128)S(1)} %copy.133), channel_id=3, replica_groups=mesh['yh'=2,'core'=2,'x'=4,'z'=4,'yl'=2] {'x','z','yl'}, use_global_device_ids=true, to_apply=%region_11.12.clone | all-reduce | flops 2880 | bytes 23040
  520.4 3.2 collective-permute-start.5
  531.4 3.2 collective-permute-start.21
  537.9 15.0 %psum.21 = f32[2,4,1920]{2,1,0:T(4,128)S(1)} all-reduce(f32[2,4,1920]{2,1,0:T(4,128)S(1)} %pad_maximum_fusion.14), channel_id=1, replica_groups=mesh['yh'=2,'core'=2,'x'=4,'z'=4,'yl'=2] {'x'}, use_global_device_ids=true, to_apply=%region_0.1 | all-reduce | flops 15360 | bytes 122880 | tf_op jit(solution)/shard_map/psum | solution.py:135
  553.0 15.1 %psum.22 = f32[2,4,1920]{2,1,0:T(4,128)S(1)} all-reduce(f32[2,4,1920]{2,1,0:T(4,128)S(1)} %psum.21), channel_id=1, replica_groups=mesh['yh'=2,'core'=2,'x'=4,'z'=4,'yl'=2] {'z'}, use_global_device_ids=true, to_apply=%region_1.2 | all-reduce | flops 15360 | bytes 122880 | tf_op jit(solution)/shard_map/psum | solution.py:135
  581.2 2.7 collective-permute-start.22
  583.9 3.9 collective-permute-done.4
  589.8 2.6 collective-permute-start.9
  596.0 3.2 collective-permute-start.25
  600.1 3.1 collective-permute-start.10
  603.4 3.3 collective-permute-start.26
  607.3 3.5 collective-permute-done.24
  614.8 3.3 collective-permute-start.27
  618.8 2.6 collective-permute-start.11
  628.5 65.5 %psum.23 = f32[3]{0:T(128)S(1)} all-reduce(f32[3]{0:T(128)S(1)} %pad_maximum_fusion.17), channel_id=1, replica_groups=mesh['yh'=2,'core'=2,'x'=4,'z'=4,'yl'=2] {'yh','core','x','z','yl'}, use_global_device_ids=true, to_apply=%region_18.19 | all-reduce | flops 3 | bytes 24 | tf_op jit(solution)/shard_map/psum | solution.py:169
  712.0 2.7 collective-permute-start.31
  718.4 2.7 collective-permute-start.15
  721.1 3.1 fusion.43
  724.2 2.9 fusion.69
  728.3 7.1 collective-permute-done.32
  735.6 3.3 collective-permute-start.34
  742.9 3.2 collective-permute-start.18
  766.1 3.0 copy.121
  769.1 2.6 fusion.32
  781.5 6.9 collective-permute-done.35
  (299 shorter events, 134.1 us)
Async XLA Ops:
  7.2 7.7 copy-start.42
  7.2 347.3 %all-reduce.4.cloned.1.call-start = ((), (), s32[]{:S(2)}) async-start(), calls=%async_computation | async-start | bytes 262144
  13.2 113.1 %collective-permute-start.1 = (bf16[375,1920]{1,0:T(8,128)(2,1)}, bf16[375,1920]{1,0:T(8,128)(2,1)}, u32[]{:S(2)}, u32[]{:S(2)}) collective-permute-start(bf16[375,1920]{1,0:T(8,128)(2,1)} %dynamic-slice_bitcast_fusion), channel_id=1, source_target_pairs={{0,1},{1,0},{32,97},{33,96},{64,65},{65,64},{96,33},{97,32},{2,3},... | collective-permute-start | bytes 4320008 | tf_op jit(solution)/shard_map/ppermute | solution.py:82
  26.3 485.4 %collective-permute-start = (bf16[1024,375]{0,1:T(8,128)(2,1)}, bf16[1024,375]{0,1:T(8,128)(2,1)}, u32[]{:S(2)}, u32[]{:S(2)}) collective-permute-start(bf16[1024,375]{0,1:T(8,128)(2,1)} %copy.104), channel_id=1, source_target_pairs={{0,1},{1,0},{32,97},{33,96},{64,65},{65,64},{96,33},{97,32},{2,3},... | collective-permute-start | bytes 2304008 | tf_op jit(solution)/shard_map/ppermute | solution.py:82
  26.7 510.6 %collective-permute-start.36 = (bf16[4,375]{1,0:T(4,128)(2,1)S(1)}, bf16[4,375]{1,0:T(4,128)(2,1)S(1)}, u32[]{:S(2)}, u32[]{:S(2)}) collective-permute-start(bf16[4,375]{1,0:T(4,128)(2,1)S(1)} %reshape.436), channel_id=1, source_target_pairs={{0,1},{1,0},{2,3},{3,2},{4,5},{5,4},{6,7},{7,6},{8,9},{9,8},{10,11... | collective-permute-start | bytes 9008 | tf_op jit(solution)/shard_map/ppermute | solution.py:127
  126.3 387.9 %collective-permute-start.2 = (bf16[375,1920]{1,0:T(8,128)(2,1)}, bf16[375,1920]{1,0:T(8,128)(2,1)}, u32[]{:S(2)}, u32[]{:S(2)}) collective-permute-start(bf16[375,1920]{1,0:T(8,128)(2,1)} %collective-permute-done.1), channel_id=1, source_target_pairs={{0,32},{32,0},{1,33},{33,1},{2,34},{34,2},{3,35},{35,3},{4,36},{36... | collective-permute-start | bytes 4320008 | tf_op jit(solution)/shard_map/ppermute | solution.py:85
  514.1 21.9 %copy-start.25 = (bf16[4,4,64,375]{3,2,1,0:T(8,128)(2,1)}, bf16[4,4,64,375]{3,2,1,0:T(8,128)(2,1)S(1)}, u32[]{:S(2)}) copy-start(bf16[4,4,64,375]{3,2,1,0:T(8,128)(2,1)S(1)} %copy.118) | copy-start | bytes 2304004
  518.0 52.1 %collective-permute-start.3 = (bf16[128,1920]{1,0:T(8,128)(2,1)}, bf16[128,1920]{1,0:T(8,128)(2,1)}, u32[]{:S(2)}, u32[]{:S(2)}) collective-permute-start(bf16[128,1920]{1,0:T(8,128)(2,1)} %fusion.13), channel_id=1, source_target_pairs={{0,8},{8,16},{16,24},{24,0},{1,9},{9,17},{17,25},{25,1},{2,10},{10... | collective-permute-start | bytes 1474568 | tf_op jit(solution)/shard_map/ppermute | solution.py:22
  520.4 51.8 %collective-permute-start.5 = (bf16[128,1920]{1,0:T(8,128)(2,1)}, bf16[128,1920]{1,0:T(8,128)(2,1)}, u32[]{:S(2)}, u32[]{:S(2)}) collective-permute-start(bf16[128,1920]{1,0:T(8,128)(2,1)} %fusion.17), channel_id=1, source_target_pairs={{0,24},{8,0},{16,8},{24,16},{1,25},{9,1},{17,9},{25,17},{2,26},{10... | collective-permute-start | bytes 1474568 | tf_op jit(solution)/shard_map/ppermute | solution.py:26
  528.9 47.9 %collective-permute-start.19 = (bf16[128,1920]{1,0:T(8,128)(2,1)}, bf16[128,1920]{1,0:T(8,128)(2,1)}, u32[]{:S(2)}, u32[]{:S(2)}) collective-permute-start(bf16[128,1920]{1,0:T(8,128)(2,1)} %fusion.19), channel_id=1, source_target_pairs={{0,2},{2,4},{4,6},{6,0},{1,3},{3,5},{5,7},{7,1},{8,10},{10,12},{12... | collective-permute-start | bytes 1474568 | tf_op jit(solution)/shard_map/ppermute | solution.py:22
  531.4 48.2 %collective-permute-start.21 = (bf16[128,1920]{1,0:T(8,128)(2,1)}, bf16[128,1920]{1,0:T(8,128)(2,1)}, u32[]{:S(2)}, u32[]{:S(2)}) collective-permute-start(bf16[128,1920]{1,0:T(8,128)(2,1)} %fusion.23), channel_id=1, source_target_pairs={{0,6},{2,0},{4,2},{6,4},{1,7},{3,1},{5,3},{7,5},{8,14},{10,8},{12,... | collective-permute-start | bytes 1474568 | tf_op jit(solution)/shard_map/ppermute | solution.py:26
  571.8 16.1 %collective-permute-start.4 = (bf16[256,1920]{1,0:T(8,128)(2,1)S(1)}, bf16[256,1920]{1,0:T(8,128)(2,1)S(1)}, u32[]{:S(2)}, u32[]{:S(2)}) collective-permute-start(bf16[256,1920]{1,0:T(8,128)(2,1)S(1)} %pad_maximum_fusion.4), channel_id=1, source_target_pairs={{0,8},{8,16},{16,24},{24,0},{1,9},{9,17},{17,25},{25,1},{2,10},{10... | collective-permute-start | bytes 2949128 | tf_op jit(solution)/shard_map/ppermute | solution.py:22
  574.5 14.2 %collective-permute-start.6 = (bf16[256,1920]{1,0:T(8,128)(2,1)S(1)}, bf16[256,1920]{1,0:T(8,128)(2,1)S(1)}, u32[]{:S(2)}, u32[]{:S(2)}) collective-permute-start(bf16[256,1920]{1,0:T(8,128)(2,1)S(1)} %pad_maximum_fusion.5), channel_id=1, source_target_pairs={{0,24},{8,0},{16,8},{24,16},{1,25},{9,1},{17,9},{25,17},{2,26},{10... | collective-permute-start | bytes 2949128 | tf_op jit(solution)/shard_map/ppermute | solution.py:26
  578.5 15.8 %collective-permute-start.20 = (bf16[256,1920]{1,0:T(8,128)(2,1)S(1)}, bf16[256,1920]{1,0:T(8,128)(2,1)S(1)}, u32[]{:S(2)}, u32[]{:S(2)}) collective-permute-start(bf16[256,1920]{1,0:T(8,128)(2,1)S(1)} %pad_maximum_fusion.6), channel_id=1, source_target_pairs={{0,2},{2,4},{4,6},{6,0},{1,3},{3,5},{5,7},{7,1},{8,10},{10,12},{12... | collective-permute-start | bytes 2949128 | tf_op jit(solution)/shard_map/ppermute | solution.py:22
  581.1 7.6 copy-start.23
  581.1 7.5 copy-start.24
  581.2 14.3 %collective-permute-start.22 = (bf16[256,1920]{1,0:T(8,128)(2,1)S(1)}, bf16[256,1920]{1,0:T(8,128)(2,1)S(1)}, u32[]{:S(2)}, u32[]{:S(2)}) collective-permute-start(bf16[256,1920]{1,0:T(8,128)(2,1)S(1)} %pad_maximum_fusion.7), channel_id=1, source_target_pairs={{0,6},{2,0},{4,2},{6,4},{1,7},{3,1},{5,3},{7,5},{8,14},{10,8},{12,... | collective-permute-start | bytes 2949128 | tf_op jit(solution)/shard_map/ppermute | solution.py:26
  589.1 6.5 copy-start.19
  589.1 10.1 %collective-permute-start.7 = (bf16[32,1920]{1,0:T(8,128)(2,1)S(1)}, bf16[32,1920]{1,0:T(8,128)(2,1)S(1)}, u32[]{:S(2)}, u32[]{:S(2)}) collective-permute-start(bf16[32,1920]{1,0:T(8,128)(2,1)S(1)} %get-tuple-element.50), channel_id=1, source_target_pairs={{0,2},{2,4},{4,6},{6,0},{1,3},{3,5},{5,7},{7,1},{8,10},{10,12},{12... | collective-permute-start | bytes 368648 | tf_op jit(solution)/shard_map/ppermute | solution.py:22
  589.8 9.5 %collective-permute-start.9 = (bf16[32,1920]{1,0:T(8,128)(2,1)S(1)}, bf16[32,1920]{1,0:T(8,128)(2,1)S(1)}, u32[]{:S(2)}, u32[]{:S(2)}) collective-permute-start(bf16[32,1920]{1,0:T(8,128)(2,1)S(1)} %get-tuple-element.51), channel_id=1, source_target_pairs={{0,6},{2,0},{4,2},{6,4},{1,7},{3,1},{5,3},{7,5},{8,14},{10,8},{12,... | collective-permute-start | bytes 368648 | tf_op jit(solution)/shard_map/ppermute | solution.py:26
  596.0 7.3 collective-permute-start.23
  596.0 7.2 collective-permute-start.25
  599.4 7.9 collective-permute-start.8
  600.1 7.2 collective-permute-start.10
  603.3 7.5 collective-permute-start.24
  603.4 7.4 collective-permute-start.26
  614.8 82.8 %collective-permute-start.27 = (bf16[64,1920]{1,0:T(8,128)(2,1)}, bf16[64,1920]{1,0:T(8,128)(2,1)}, u32[]{:S(2)}, u32[]{:S(2)}) collective-permute-start(bf16[64,1920]{1,0:T(8,128)(2,1)} %get-tuple-element.30), channel_id=1, source_target_pairs={{0,24},{8,0},{16,8},{24,16},{1,25},{9,1},{17,9},{25,17},{2,26},{10... | collective-permute-start | bytes 737288 | tf_op jit(solution)/shard_map/ppermute | solution.py:26
  618.1 76.7 %collective-permute-start.28 = (bf16[64,1920]{1,0:T(8,128)(2,1)}, bf16[64,1920]{1,0:T(8,128)(2,1)}, u32[]{:S(2)}, u32[]{:S(2)}) collective-permute-start(bf16[64,1920]{1,0:T(8,128)(2,1)} %get-tuple-element.30), channel_id=1, source_target_pairs={{0,8},{8,16},{16,24},{24,0},{1,9},{9,17},{17,25},{25,1},{2,10},{10... | collective-permute-start | bytes 737288 | tf_op jit(solution)/shard_map/ppermute | solution.py:22
  618.8 83.9 %collective-permute-start.11 = (bf16[64,1920]{1,0:T(8,128)(2,1)S(1)}, bf16[64,1920]{1,0:T(8,128)(2,1)}, u32[]{:S(2)}, u32[]{:S(2)}) collective-permute-start(bf16[64,1920]{1,0:T(8,128)(2,1)S(1)} %get-tuple-element.58), channel_id=1, source_target_pairs={{0,6},{2,0},{4,2},{6,4},{1,7},{3,1},{5,3},{7,5},{8,14},{10,8},{12,... | collective-permute-start | bytes 737288 | tf_op jit(solution)/shard_map/ppermute | solution.py:26
  621.4 78.6 %collective-permute-start.12 = (bf16[64,1920]{1,0:T(8,128)(2,1)S(1)}, bf16[64,1920]{1,0:T(8,128)(2,1)}, u32[]{:S(2)}, u32[]{:S(2)}) collective-permute-start(bf16[64,1920]{1,0:T(8,128)(2,1)S(1)} %get-tuple-element.58), channel_id=1, source_target_pairs={{0,2},{2,4},{4,6},{6,0},{1,3},{3,5},{5,7},{7,1},{8,10},{10,12},{12... | collective-permute-start | bytes 737288 | tf_op jit(solution)/shard_map/ppermute | solution.py:22
  628.5 65.7 %collective-permute-start.37 = (f32[2,15]{1,0:T(2,128)S(1)}, f32[2,15]{1,0:T(2,128)S(1)}, u32[]{:S(2)}, u32[]{:S(2)}) collective-permute-start(f32[2,15]{1,0:T(2,128)S(1)} %constant_dynamic-slice_fusion), channel_id=1, source_target_pairs={{0,1},{1,0},{2,3},{3,2},{4,5},{5,4},{6,7},{7,6},{8,9},{9,8},{10,11... | collective-permute-start | bytes 368 | tf_op jit(solution)/shard_map/ppermute | solution.py:180
  695.7 12.8 %collective-permute-start.29 = (bf16[32,1920]{1,0:T(8,128)(2,1)S(1)}, bf16[32,1920]{1,0:T(8,128)(2,1)S(1)}, u32[]{:S(2)}, u32[]{:S(2)}) collective-permute-start(bf16[32,1920]{1,0:T(8,128)(2,1)S(1)} %slice.420), channel_id=1, source_target_pairs={{0,8},{8,16},{16,24},{24,0},{1,9},{9,17},{17,25},{25,1},{2,10},{10... | collective-permute-start | bytes 368648 | tf_op jit(solution)/shard_map/ppermute | solution.py:22
  698.4 10.8 %collective-permute-start.30 = (bf16[32,1920]{1,0:T(8,128)(2,1)S(1)}, bf16[32,1920]{1,0:T(8,128)(2,1)S(1)}, u32[]{:S(2)}, u32[]{:S(2)}) collective-permute-start(bf16[32,1920]{1,0:T(8,128)(2,1)S(1)} %slice.421), channel_id=1, source_target_pairs={{0,24},{8,0},{16,8},{24,16},{1,25},{9,1},{17,9},{25,17},{2,26},{10... | collective-permute-start | bytes 368648 | tf_op jit(solution)/shard_map/ppermute | solution.py:26
  700.9 13.8 %collective-permute-start.13 = (bf16[32,1920]{1,0:T(8,128)(2,1)S(1)}, bf16[32,1920]{1,0:T(8,128)(2,1)S(1)}, u32[]{:S(2)}, u32[]{:S(2)}) collective-permute-start(bf16[32,1920]{1,0:T(8,128)(2,1)S(1)} %slice.392), channel_id=1, source_target_pairs={{0,2},{2,4},{4,6},{6,0},{1,3},{3,5},{5,7},{7,1},{8,10},{10,12},{12... | collective-permute-start | bytes 368648 | tf_op jit(solution)/shard_map/ppermute | solution.py:22
  703.6 11.8 %collective-permute-start.14 = (bf16[32,1920]{1,0:T(8,128)(2,1)S(1)}, bf16[32,1920]{1,0:T(8,128)(2,1)S(1)}, u32[]{:S(2)}, u32[]{:S(2)}) collective-permute-start(bf16[32,1920]{1,0:T(8,128)(2,1)S(1)} %slice.393), channel_id=1, source_target_pairs={{0,6},{2,0},{4,2},{6,4},{1,7},{3,1},{5,3},{7,5},{8,14},{10,8},{12,... | collective-permute-start | bytes 368648 | tf_op jit(solution)/shard_map/ppermute | solution.py:26
  711.5 23.9 %collective-permute-start.32 = (bf16[256,1920]{1,0:T(8,128)(2,1)}, bf16[256,1920]{1,0:T(8,128)(2,1)S(1)}, u32[]{:S(2)}, u32[]{:S(2)}) collective-permute-start(bf16[256,1920]{1,0:T(8,128)(2,1)} %constant_dynamic-update-slice_fusion.7), channel_id=1, source_target_pairs={{0,2},{2,4},{4,6},{6,0},{1,3},{3,5},{5,7},{7,1},{8,10},{10,12},{12... | collective-permute-start | bytes 2949128 | tf_op jit(solution)/shard_map/ppermute | solution.py:22
  712.0 23.5 %collective-permute-start.31 = (bf16[256,1920]{1,0:T(8,128)(2,1)}, bf16[256,1920]{1,0:T(8,128)(2,1)S(1)}, u32[]{:S(2)}, u32[]{:S(2)}) collective-permute-start(bf16[256,1920]{1,0:T(8,128)(2,1)} %constant_dynamic-update-slice_fusion.7), channel_id=1, source_target_pairs={{0,6},{2,0},{4,2},{6,4},{1,7},{3,1},{5,3},{7,5},{8,14},{10,8},{12,... | collective-permute-start | bytes 2949128 | tf_op jit(solution)/shard_map/ppermute | solution.py:26
  717.7 6.5 copy-start.6
  717.7 23.5 %collective-permute-start.16 = (bf16[256,1920]{1,0:T(8,128)(2,1)}, bf16[256,1920]{1,0:T(8,128)(2,1)S(1)}, u32[]{:S(2)}, u32[]{:S(2)}) collective-permute-start(bf16[256,1920]{1,0:T(8,128)(2,1)} %constant_dynamic-update-slice_fusion), channel_id=1, source_target_pairs={{0,8},{8,16},{16,24},{24,0},{1,9},{9,17},{17,25},{25,1},{2,10},{10... | collective-permute-start | bytes 2949128 | tf_op jit(solution)/shard_map/ppermute | solution.py:22
  718.4 23.6 %collective-permute-start.15 = (bf16[256,1920]{1,0:T(8,128)(2,1)}, bf16[256,1920]{1,0:T(8,128)(2,1)S(1)}, u32[]{:S(2)}, u32[]{:S(2)}) collective-permute-start(bf16[256,1920]{1,0:T(8,128)(2,1)} %constant_dynamic-update-slice_fusion), channel_id=1, source_target_pairs={{0,24},{8,0},{16,8},{24,16},{1,25},{9,1},{17,9},{25,17},{2,26},{10... | collective-permute-start | bytes 2949128 | tf_op jit(solution)/shard_map/ppermute | solution.py:26
  721.1 6.0 copy-start.5
  724.2 25.9 %slice-start = ((s8[8663040]{0:T(1024)(128)(4,1)}), s8[4194304]{0:T(1024)(128)(4,1)S(1)}, s32[]{:S(2)}) async-start(s8[8663040]{0:T(1024)(128)(4,1)} %bitcast.415), calls=%async_computation.1 | async-start | bytes 8388608
  727.7 22.4 %slice-start.1 = ((s8[8663040]{0:T(1024)(128)(4,1)}), s8[4194304]{0:T(1024)(128)(4,1)S(1)}, s32[]{:S(2)}) async-start(s8[8663040]{0:T(1024)(128)(4,1)} %bitcast.415), calls=%async_computation.2 | async-start | bytes 8388608
  735.5 20.1 %collective-permute-start.33 = (bf16[128,1920]{1,0:T(8,128)(2,1)S(1)}, bf16[128,1920]{1,0:T(8,128)(2,1)S(1)}, u32[]{:S(2)}, u32[]{:S(2)}) collective-permute-start(bf16[128,1920]{1,0:T(8,128)(2,1)S(1)} %slice.422), channel_id=1, source_target_pairs={{0,2},{2,4},{4,6},{6,0},{1,3},{3,5},{5,7},{7,1},{8,10},{10,12},{12... | collective-permute-start | bytes 1474568 | tf_op jit(solution)/shard_map/ppermute | solution.py:22
  735.6 20.0 %collective-permute-start.34 = (bf16[128,1920]{1,0:T(8,128)(2,1)S(1)}, bf16[128,1920]{1,0:T(8,128)(2,1)S(1)}, u32[]{:S(2)}, u32[]{:S(2)}) collective-permute-start(bf16[128,1920]{1,0:T(8,128)(2,1)S(1)} %slice.423), channel_id=1, source_target_pairs={{0,6},{2,0},{4,2},{6,4},{1,7},{3,1},{5,3},{7,5},{8,14},{10,8},{12,... | collective-permute-start | bytes 1474568 | tf_op jit(solution)/shard_map/ppermute | solution.py:26
  742.1 18.4 %collective-permute-start.17 = (bf16[128,1920]{1,0:T(8,128)(2,1)}, bf16[128,1920]{1,0:T(8,128)(2,1)}, u32[]{:S(2)}, u32[]{:S(2)}) collective-permute-start(bf16[128,1920]{1,0:T(8,128)(2,1)} %slice.394), channel_id=1, source_target_pairs={{0,8},{8,16},{16,24},{24,0},{1,9},{9,17},{17,25},{25,1},{2,10},{10... | collective-permute-start | bytes 1474568 | tf_op jit(solution)/shard_map/ppermute | solution.py:22
  742.9 18.7 %collective-permute-start.18 = (bf16[128,1920]{1,0:T(8,128)(2,1)}, bf16[128,1920]{1,0:T(8,128)(2,1)}, u32[]{:S(2)}, u32[]{:S(2)}) collective-permute-start(bf16[128,1920]{1,0:T(8,128)(2,1)} %slice.395), channel_id=1, source_target_pairs={{0,24},{8,0},{16,8},{24,16},{1,25},{9,1},{17,9},{25,17},{2,26},{10... | collective-permute-start | bytes 1474568 | tf_op jit(solution)/shard_map/ppermute | solution.py:26
  771.7 16.7 %collective-permute-start.35 = (bf16[4,4,64,375]{3,2,1,0:T(8,128)(2,1)}, bf16[4,4,64,375]{3,2,1,0:T(8,128)(2,1)}, u32[]{:S(2)}, u32[]{:S(2)}) collective-permute-start(bf16[4,4,64,375]{3,2,1,0:T(8,128)(2,1)} %fusion.32), channel_id=1, source_target_pairs={{0,1},{1,0},{2,3},{3,2},{4,5},{5,4},{6,7},{7,6},{8,9},{9,8},{10,11... | collective-permute-start | bytes 2304008 | tf_op jit(solution)/shard_map/ppermute | solution.py:193
  (39 other events, 101.1 us)
Sparse Core Ops, SparseCore 0:
  73.5 280.9 all-reduce.3
